TPU v7x, 512 devices: a whole 4x4x16 slice. The times are simulated.
512 devices in a mesh: grp: 16 (over x, y), dev: 32 (over z, core).
Axes of the slice: x: 4, y: 4, z: 16, core: 2. Of those that a mesh axis runs over, the one named last changes fastest.
Arguments:
- records: bfloat16 [131072, 128], P('grp', 'dev')
- dropout: int32 [131072, 128], P('grp', 'dev'), may hold values 0 or 1
- counts: int32 [512], P(('grp', 'dev')), may hold values from 128 to 256, as said below
Outputs:
- upper: float32 [512, 512], replicated
- basis: bfloat16 [131072, 512], P(('grp', 'dev'))
Inputs may be any that keep to these rules, and one draw needn't show every extreme that they name: `counts`: at least one time shard has all 256 rows valid.
All inputs are finite; a program needn't handle non-finite values. No bound on the sum of `dropout` on one device may be relied on, other than what follows from the above.
Results may differ from a plain program's by a relative error of at most 0.0012.
Values may be sent and summed in bfloat16 or wider, within the bound.
No kernel may reach another device: no remote copies, remote signals or barrier semaphores. Data moves between devices by JAX's collectives and lax.ppermute only.
A program may use at most 128 MiB of HBM per device.

v0:
```python
import jax
import jax.numpy as jnp
from jax import lax
from jax.sharding import PartitionSpec as P

LAGS = 4


def from_behind(value, axis, by):
    size = lax.axis_size(axis)
    pairs = [(i, i + by) for i in range(size) if 0 <= i + by < size]
    return lax.ppermute(value, axis, pairs)


def gram_term(piece):
    return lax.dot_general(
        piece, piece, (((0,), (0,)), ((), ())), preferred_element_type=jnp.float32
    )


def project(piece, high, low):
    first = jnp.dot(piece, high, preferred_element_type=jnp.float32)
    second = jnp.dot(piece, low, preferred_element_type=jnp.float32)
    return (first + second).astype(jnp.bfloat16)


def exact_dot(left, right):
    return jnp.dot(left, right, precision=lax.Precision.HIGHEST)


def factor_block(block):
    size = block.shape[0]
    augmented = jnp.concatenate([block, jnp.eye(size, dtype=jnp.float32)], axis=1)
    order = jnp.arange(size, dtype=jnp.int32)

    def eliminate(step, state):
        working, written = state
        pivot_row = lax.dynamic_slice_in_dim(working, step, 1, 0)[0]
        pivot = lax.dynamic_slice_in_dim(pivot_row, step, 1, 0)[0]
        scaled = pivot_row / jnp.sqrt(pivot)
        column = lax.dynamic_slice_in_dim(working, step, 1, 1)[:, 0]
        factor = jnp.where(order > step, column / pivot, jnp.zeros_like(column))
        working = working - factor[:, None] * pivot_row[None, :]
        written = lax.dynamic_update_slice_in_dim(written, scaled[None, :], step, 0)
        return (working, written)

    _, written = lax.fori_loop(0, size, eliminate, (augmented, jnp.zeros_like(augmented)))
    upper_block = jnp.triu(written[:, :size])
    lower_inverse = jnp.tril(written[:, size:])
    return (upper_block, lower_inverse)


def factor_parts(matrix):
    size = matrix.shape[0]
    panel = min(128, size)
    panels = size // panel
    working = matrix
    diag_blocks = []
    diag_inverses = []
    right_blocks = []
    for number in range(panels):
        upper_block, lower_inverse = factor_block(working[:panel, :panel])
        beside = exact_dot(lower_inverse, working[:panel, panel:])
        working = working[panel:, panel:] - exact_dot(jnp.transpose(beside), beside)
        diag_blocks.append(upper_block)
        diag_inverses.append(jnp.transpose(lower_inverse))
        right_blocks.append(beside)
    block_rows = []
    for number in range(panels):
        pieces = []
        if number > 0:
            pieces.append(jnp.zeros((panel, number * panel), jnp.float32))
        pieces.append(diag_blocks[number])
        if number + 1 < panels:
            pieces.append(right_blocks[number])
        block_rows.append(jnp.concatenate(pieces, axis=1))
    upper = jnp.concatenate(block_rows, axis=0)
    solved = [[None] * panels for number in range(panels)]
    for column in range(panels):
        solved[column][column] = diag_inverses[column]
        for row in range(column - 1, -1, -1):
            accum = jnp.zeros((panel, panel), jnp.float32)
            for middle in range(row + 1, column + 1):
                coupling = upper[
                    row * panel : (row + 1) * panel, middle * panel : (middle + 1) * panel
                ]
                accum = accum + exact_dot(coupling, solved[middle][column])
            solved[row][column] = -exact_dot(diag_inverses[row], accum)
    inverse_rows = []
    for row in range(panels):
        pieces = []
        for column in range(panels):
            if column < row:
                pieces.append(jnp.zeros((panel, panel), jnp.float32))
            else:
                pieces.append(solved[row][column])
        inverse_rows.append(jnp.concatenate(pieces, axis=1))
    return (upper, jnp.concatenate(inverse_rows, axis=0))


def shards(records, dropout, counts):
    local = (records.astype(jnp.float32) * dropout.astype(jnp.float32)).astype(jnp.bfloat16)
    series = lax.all_to_all(local, "dev", split_axis=0, concat_axis=1, tiled=True)
    rows = series.shape[0]
    ahead = from_behind(series[: LAGS - 1], ("grp", "dev"), -1)
    padded = jnp.concatenate([series, ahead], axis=0)
    hankel = jnp.concatenate([padded[k : k + rows] for k in range(LAGS)], axis=1)
    valid = jnp.arange(rows, dtype=jnp.int32) >= rows - counts[0]
    hankel = jnp.where(valid[:, None], hankel, jnp.zeros_like(hankel))
    total_rows = rows * lax.axis_size("grp") * lax.axis_size("dev")
    partial_value = gram_term(hankel)
    gram = lax.psum(partial_value, ("grp", "dev"))
    upper, inverse = factor_parts(gram / total_rows)
    high = inverse.astype(jnp.bfloat16)
    low = (inverse - lax.optimization_barrier(high).astype(jnp.float32)).astype(jnp.bfloat16)
    basis = project(hankel, high, low)
    return (upper, basis)


def solution(mesh):
    in_specs = (P("grp", "dev"), P("grp", "dev"), P(("grp", "dev")))
    out_specs = (P(), P(("grp", "dev"), None))
    return jax.shard_map(shards, mesh=mesh, in_specs=in_specs, out_specs=out_specs, check_vma=False)
```

profile of v0, /device:TPU:1, one launch (start us, length us, event | category | flops | bytes accessed | tf_op | source)
XLA Modules:
  0.0 1999.9 jit_solution(4296532873974421739)
XLA Ops:
  7.2 1.6 multiply_convert_fusion
  8.7 16.8 all-to-all-start
  26.2 12.4 all-to-all-done
  38.6 3.5 collective-permute-start
  42.1 1.7 collective-permute-done
  44.0 1.3 fusion.66
  45.4 462.2 %all-reduce.3.cloned.1.call-done = f32[512,512]{1,0:T(8,128)} async-done(((f32[512,512]{1,0:T(8,128)}), f32[512,512]{1,0:T(8,128)}) %all-reduce.3.cloned.1.call-update) | async-done | bytes 1048592 | tf_op jit(solution)/shard_map/psum | solution.py:112
  507.6 1.3 broadcast_multiply_fusion
  509.1 368.6 %while.76 = (s32[]{:T(128)}, f32[128,256]{0,1:T(8,128)S(1)}, f32[128,256]{0,1:T(8,128)S(1)}, s32[]{:T(128)}, s32[]{:T(128)}, /*index=5*/s32[]{:T(128)}, s32[]{:T(128)}) while((s32[]{:T(128)}, f32[128,256]{0,1:T(8,128)S(1)}, f32[128,256]{0,1:T(8,128)S(1)}, s32[]{:T(128)}, s32[]{:T(128)}, /*index=5*/s32[]{:T(128)}, s32[]{:T(128)}) %tuple.188), condition=%wide.region_2.3_spmd.clone, body=%wide.region_1.2_spmd.clone.sunk | while | flops 66180 | bytes 271501 | solution.py:47
  513.9 0.7 fusion.92
  522.6 0.7 fusion.92
  531.2 0.7 fusion.92
  539.8 0.7 fusion.92
  542.7 0.7 fusion.92
  548.5 0.7 fusion.92
  551.4 0.7 fusion.92
  560.0 0.7 fusion.92
  568.7 0.7 fusion.92
  577.3 0.7 fusion.92
  585.9 0.7 fusion.92
  594.6 0.7 fusion.92
  597.5 0.7 fusion.92
  603.2 0.7 fusion.92
  606.1 0.7 fusion.92
  614.7 0.7 fusion.92
  623.4 0.7 fusion.92
  878.0 0.7 convolution_subtract_fusion
  878.9 368.6 %while.77 = (s32[]{:T(128)}, f32[128,256]{0,1:T(8,128)S(1)}, f32[128,256]{0,1:T(8,128)S(1)}, s32[]{:T(128)}, s32[]{:T(128)}, /*index=5*/s32[]{:T(128)}, s32[]{:T(128)}) while((s32[]{:T(128)}, f32[128,256]{0,1:T(8,128)S(1)}, f32[128,256]{0,1:T(8,128)S(1)}, s32[]{:T(128)}, s32[]{:T(128)}, /*index=5*/s32[]{:T(128)}, s32[]{:T(128)}) %tuple.191), condition=%wide.region_4.5_spmd.clone, body=%wide.region_3.4_spmd.clone.sunk | while | flops 66180 | bytes 271501 | solution.py:47
  1248.6 368.6 %while.78 = (s32[]{:T(128)}, f32[128,256]{0,1:T(8,128)S(1)}, f32[128,256]{0,1:T(8,128)S(1)}, s32[]{:T(128)}, s32[]{:T(128)}, /*index=5*/s32[]{:T(128)}, s32[]{:T(128)}) while((s32[]{:T(128)}, f32[128,256]{0,1:T(8,128)S(1)}, f32[128,256]{0,1:T(8,128)S(1)}, s32[]{:T(128)}, s32[]{:T(128)}, /*index=5*/s32[]{:T(128)}, s32[]{:T(128)}) %tuple.194), condition=%wide.region_6.7_spmd.clone, body=%wide.region_5.6_spmd.clone.sunk | while | flops 66180 | bytes 271501 | solution.py:47
  1618.2 368.6 %while.79 = (s32[]{:T(128)}, f32[128,256]{0,1:T(8,128)S(1)}, f32[128,256]{0,1:T(8,128)S(1)}, s32[]{:T(128)}, s32[]{:T(128)}, /*index=5*/s32[]{:T(128)}, s32[]{:T(128)}) while((s32[]{:T(128)}, f32[128,256]{0,1:T(8,128)S(1)}, f32[128,256]{0,1:T(8,128)S(1)}, s32[]{:T(128)}, s32[]{:T(128)}, /*index=5*/s32[]{:T(128)}, s32[]{:T(128)}) %tuple.197), condition=%wide.region_8.9_spmd.clone, body=%wide.region_7.8_spmd.clone.sunk | while | flops 66180 | bytes 271501 | solution.py:47
  1990.8 1.1 fusion.12
  1992.0 1.1 fusion.16
  (2601 shorter events, 1093.3 us)
Async XLA Ops:
  8.7 29.8 %all-to-all-start = ((bf16[32,256,4]{1,2,0:T(4,128)(2,1)}), bf16[32,256,4]{1,2,0:T(4,128)(2,1)S(1)}, u32[]{:S(2)}, u32[]{:S(2)}) async-start(bf16[32,256,4]{1,2,0:T(4,128)(2,1)} %bitcast.1), calls=%async_computation | async-start | bytes 131072 | tf_op jit(solution)/shard_map/all_to_all | solution.py:103
  25.5 482.1 %all-reduce.3.cloned.1.call-start = ((), (), s32[]{:S(2)}) async-start(), calls=%async_computation.1 | async-start | bytes 2097152 | tf_op jit(solution)/shard_map/psum | solution.py:112
  38.6 5.2 collective-permute-start
Sparse Core Ops, SparseCore 0:
  45.4 462.1 all-reduce.2
where the time goes:
time: 2020 us; the launch traced here: 2000 us
  local copies, waits for them, and re-layouts  614 us (30%)
  other arithmetic  489 us (24%)
  waiting for transfers between devices  476 us (24%)
  loops' own time  377 us (19%)
  starting transfers between devices  20.3 us (1%)
    psum x1, waiting for transfers between devices, shards(): gram = lax.psum(partial_value, ('grp', 'dev'))  462 us
    another operation x4, loops' own time, factor_block(): lax.fori_loop(0, size, eliminate, (augmented, jnp.zeros_like(augmented)))  377 us
    mul x512, other arithmetic, eliminate(): working = working - factor[:, None] * pivot_row[None, :]  337 us
    dynamic_update_slice x512, local copies, waits for them, and re-layouts, eliminate(): written = lax.dynamic_update_slice_in_dim(written, scaled[None, :], step, 0)  312 us
    dynamic_slice x512, local copies, waits for them, and re-layouts, eliminate(): pivot = lax.dynamic_slice_in_dim(pivot_row, step, 1, 0)[0]  301 us
    div x512, other arithmetic, eliminate(): scaled = pivot_row / jnp.sqrt(pivot)  94.6 us
    sub x512, other arithmetic, eliminate(): working = working - factor[:, None] * pivot_row[None, :]  53.9 us
  transfers between devices with their start and end apart: 3, of which 3 were waited for; matrix products, arithmetic and copies ran while one was open for 0% of the time, Pallas kernels for 0%

commit v1 on v0

--- a/solution.py
+++ b/solution.py
@@ -109,7 +109,8 @@
     hankel = jnp.where(valid[:, None], hankel, jnp.zeros_like(hankel))
     total_rows = rows * lax.axis_size("grp") * lax.axis_size("dev")
     partial_value = gram_term(hankel)
-    gram = lax.psum(partial_value, ("grp", "dev"))
+    inner = lax.psum(partial_value, "dev")
+    gram = lax.psum(inner, "grp")
     upper, inverse = factor_parts(gram / total_rows)
     high = inverse.astype(jnp.bfloat16)
     low = (inverse - lax.optimization_barrier(high).astype(jnp.float32)).astype(jnp.bfloat16)

time: 2020 us -> 1870 us (0.926)
  waiting for transfers between devices: 476 us -> 339 us
    psum x1 -> x2, waiting for transfers between devices: 462 us -> 325 us  [the longest x1 206 us: shards(): inner = lax.psum(partial_value, 'dev')]
  transfers between devices with their start and end apart: 3 -> 4, of which waited for: 3 -> 4; matrix products, arithmetic and copies ran while one was open for 0% -> 0% of each run, Pallas kernels for 0% -> 0%
where the time goes in v1:
time: 1870 us; the launch traced here: 1860 us
  local copies, waits for them, and re-layouts  618 us (33%)
  other arithmetic  484 us (26%)
  loops' own time  372 us (20%)
  waiting for transfers between devices  339 us (18%)
  starting transfers between devices  20.3 us (1%)
    another operation x4, loops' own time, factor_block(): lax.fori_loop(0, size, eliminate, (augmented, jnp.zeros_like(augmented)))  372 us
    mul x512, other arithmetic, eliminate(): working = working - factor[:, None] * pivot_row[None, :]  331 us
    dynamic_update_slice x512, local copies, waits for them, and re-layouts, eliminate(): written = lax.dynamic_update_slice_in_dim(written, scaled[None, :], step, 0)  312 us
    dynamic_slice x512, local copies, waits for them, and re-layouts, eliminate(): pivot = lax.dynamic_slice_in_dim(pivot_row, step, 1, 0)[0]  305 us
    psum x1, waiting for transfers between devices, shards(): inner = lax.psum(partial_value, 'dev')  206 us
    psum x1, waiting for transfers between devices, shards(): gram = lax.psum(inner, 'grp')  120 us
    div x512, other arithmetic, eliminate(): scaled = pivot_row / jnp.sqrt(pivot)  94.6 us
    sub x512, other arithmetic, eliminate(): working = working - factor[:, None] * pivot_row[None, :]  53.9 us
  transfers between devices with their start and end apart: 4, of which 4 were waited for; matrix products, arithmetic and copies ran while one was open for 0% of the time, Pallas kernels for 0%

profile of v1, /device:TPU:1, one launch (start us, length us, event | category | flops | bytes accessed | tf_op | source)
XLA Modules:
  0.0 1856.8 jit_solution(18017949488529937172)
XLA Ops:
  7.2 1.6 multiply_convert_fusion
  8.7 16.8 all-to-all-start
  26.2 12.4 all-to-all-done
  38.6 3.5 collective-permute-start
  42.1 1.7 collective-permute-done
  44.0 1.3 fusion.66
  45.4 205.5 %all-reduce.4.cloned.1.call-done = f32[512,512]{1,0:T(8,128)} async-done(((f32[512,512]{1,0:T(8,128)}), f32[512,512]{1,0:T(8,128)}) %all-reduce.4.cloned.1.call-update) | async-done | bytes 1048592 | tf_op jit(solution)/shard_map/psum | solution.py:112
  251.0 119.6 %all-reduce.6.cloned.1.call-done = f32[512,512]{1,0:T(8,128)} async-done(((f32[512,512]{1,0:T(8,128)}), f32[512,512]{1,0:T(8,128)}) %all-reduce.6.cloned.1.call-update) | async-done | bytes 1048592 | tf_op jit(solution)/shard_map/psum | solution.py:113
  370.5 1.3 broadcast_multiply_fusion
  372.0 362.4 %while.76 = (s32[]{:T(128)}, f32[128,256]{0,1:T(8,128)S(1)}, f32[128,256]{0,1:T(8,128)S(1)}, s32[]{:T(128)}, s32[]{:T(128)}, /*index=5*/s32[]{:T(128)}, s32[]{:T(128)}) while((s32[]{:T(128)}, f32[128,256]{0,1:T(8,128)S(1)}, f32[128,256]{0,1:T(8,128)S(1)}, s32[]{:T(128)}, s32[]{:T(128)}, /*index=5*/s32[]{:T(128)}, s32[]{:T(128)}) %tuple.188), condition=%wide.region_3.4_spmd.clone, body=%wide.region_2.3_spmd.clone.sunk | while | flops 66180 | bytes 271501 | solution.py:47
  734.9 0.7 convolution_subtract_fusion
  735.7 368.6 %while.77 = (s32[]{:T(128)}, f32[128,256]{0,1:T(8,128)S(1)}, f32[128,256]{0,1:T(8,128)S(1)}, s32[]{:T(128)}, s32[]{:T(128)}, /*index=5*/s32[]{:T(128)}, s32[]{:T(128)}) while((s32[]{:T(128)}, f32[128,256]{0,1:T(8,128)S(1)}, f32[128,256]{0,1:T(8,128)S(1)}, s32[]{:T(128)}, s32[]{:T(128)}, /*index=5*/s32[]{:T(128)}, s32[]{:T(128)}) %tuple.191), condition=%wide.region_5.6_spmd.clone, body=%wide.region_4.5_spmd.clone.sunk | while | flops 66180 | bytes 271501 | solution.py:47
  737.7 0.7 fusion.93
  746.3 0.7 fusion.93
  752.1 0.7 fusion.93
  760.7 0.7 fusion.93
  769.3 0.7 fusion.93
  775.1 0.7 fusion.93
  778.0 0.7 fusion.93
  783.7 0.7 fusion.93
  792.4 0.7 fusion.93
  801.0 0.7 fusion.93
  806.8 0.7 fusion.93
  815.4 0.7 fusion.93
  824.1 0.7 fusion.93
  829.8 0.7 fusion.93
  832.7 0.7 fusion.93
  838.5 0.7 fusion.93
  1105.4 368.6 %while.78 = (s32[]{:T(128)}, f32[128,256]{0,1:T(8,128)S(1)}, f32[128,256]{0,1:T(8,128)S(1)}, s32[]{:T(128)}, s32[]{:T(128)}, /*index=5*/s32[]{:T(128)}, s32[]{:T(128)}) while((s32[]{:T(128)}, f32[128,256]{0,1:T(8,128)S(1)}, f32[128,256]{0,1:T(8,128)S(1)}, s32[]{:T(128)}, s32[]{:T(128)}, /*index=5*/s32[]{:T(128)}, s32[]{:T(128)}) %tuple.194), condition=%wide.region_7.8_spmd.clone, body=%wide.region_6.7_spmd.clone.sunk | while | flops 66180 | bytes 271501 | solution.py:47
  1475.0 368.6 %while.79 = (s32[]{:T(128)}, f32[128,256]{0,1:T(8,128)S(1)}, f32[128,256]{0,1:T(8,128)S(1)}, s32[]{:T(128)}, s32[]{:T(128)}, /*index=5*/s32[]{:T(128)}, s32[]{:T(128)}) while((s32[]{:T(128)}, f32[128,256]{0,1:T(8,128)S(1)}, f32[128,256]{0,1:T(8,128)S(1)}, s32[]{:T(128)}, s32[]{:T(128)}, /*index=5*/s32[]{:T(128)}, s32[]{:T(128)}) %tuple.197), condition=%wide.region_9.10_spmd.clone, body=%wide.region_8.9_spmd.clone.sunk | while | flops 66180 | bytes 271501 | solution.py:47
  1847.7 1.1 fusion.12
  1848.8 1.1 fusion.16
  (2604 shorter events, 1092.8 us)
Async XLA Ops:
  8.7 29.8 %all-to-all-start = ((bf16[32,256,4]{1,2,0:T(4,128)(2,1)}), bf16[32,256,4]{1,2,0:T(4,128)(2,1)S(1)}, u32[]{:S(2)}, u32[]{:S(2)}) async-start(bf16[32,256,4]{1,2,0:T(4,128)(2,1)} %bitcast.1), calls=%async_computation | async-start | bytes 131072 | tf_op jit(solution)/shard_map/all_to_all | solution.py:103
  25.5 225.4 %all-reduce.4.cloned.1.call-start = ((), (), s32[]{:S(2)}) async-start(), calls=%async_computation.1 | async-start | bytes 2097152 | tf_op jit(solution)/shard_map/psum | solution.py:112
  38.6 5.2 collective-permute-start
  45.3 325.2 %all-reduce.6.cloned.1.call-start = ((), (), s32[]{:S(2)}) async-start(), calls=%async_computation.2 | async-start | bytes 2097152 | tf_op jit(solution)/shard_map/psum | solution.py:113
Sparse Core Ops, SparseCore 0:
  45.4 205.4 all-reduce.3
  254.5 116.0 all-reduce.5
